TPU v7x, 256 devices: a whole 4x4x8 slice. The times are simulated.
256 devices in a mesh: ctx: 32 (over x, z), head: 8 (over y, core).
Axes of the slice: x: 4, y: 4, z: 8, core: 2. Of those that a mesh axis runs over, the one named last changes fastest.
Arguments:
- queries: bfloat16 [16384, 4096], P('ctx', 'head'), may hold values from -5 to 5
- key_rows: bfloat16 [16384, 1024], P('ctx', 'head'), may hold values from -5 to 5
- value_rows: bfloat16 [16384, 1024], P('ctx', 'head'), may hold values from -6 to 6
- slash_offsets: int32 [32, 4], P('head'), may hold values from 0 to 8, as said below
- union_blocks: int32 [8, 32, 2], P('head'), may hold values from 0 to 7, as said below
- head_picks: int32 [32, 32, 1], P('head'), may hold values from 0 to 1, as said below
- owner_counts: int32 [32, 32], P('head'), may hold values from 0 to 1, as said below
- out_weight: bfloat16 [4096, 4096], P(None, 'head'), may hold values from -0.09375 to 0.09375
Outputs:
- projected: bfloat16 [16384, 4096], P('ctx', 'head')
Inputs may be any that keep to these rules, and one draw needn't show every extreme that they name: `slash_offsets`: each head's offsets are distinct and include 0 and 8. `union_blocks`: the 2 entries of each KV head and sequence block are distinct. `head_picks`: the 1 entries of each query head and sequence block are distinct. `owner_counts`: equal to 1 for sequence block 0.
All inputs are finite; a program needn't handle non-finite values.
Results may differ from a plain program's by a relative error of at most 0.0056.
Values may be sent and summed in bfloat16 or wider, within the bound.
A program may use at most 128 MiB of HBM per device.

v0:
```python
import jax
import jax.numpy as jnp
from jax import lax
from jax.sharding import PartitionSpec as P

HEAD_SIZE = 128
BLOCK_TOKENS = 64
NS = 4
VPER = 1


def from_behind(array, axis, by):
    length = lax.axis_size(axis)
    pairs = [(i, i + by) for i in range(length) if 0 <= i + by < length]
    return lax.ppermute(array, axis, pairs)


def attend(
    vert_scores, vert_mask, diagonal_scores, slash_mask, vert_values, diagonal_values, per_dev
):
    masked_vert = jnp.where(vert_mask, vert_scores, -1e30)
    masked_slash = jnp.where(slash_mask, diagonal_scores, -1e30)
    peak = jnp.maximum(
        jnp.max(masked_vert, axis=-1, keepdims=True), jnp.max(masked_slash, axis=-1, keepdims=True)
    )
    weight_vert = jnp.exp(masked_vert - peak)
    weight_slash = jnp.exp(masked_slash - peak)
    total = jnp.sum(weight_vert, axis=-1, keepdims=True) + jnp.sum(
        weight_slash, axis=-1, keepdims=True
    )
    prob_vert = weight_vert.astype(jnp.bfloat16)
    slash_probability = weight_slash.astype(jnp.bfloat16).reshape(
        per_dev, BLOCK_TOKENS, NS, BLOCK_TOKENS
    )
    numer = jnp.dot(prob_vert, vert_values, preferred_element_type=jnp.float32)
    diagonal_portion = jnp.einsum(
        "wojf,wjfl->wol", slash_probability, diagonal_values, preferred_element_type=jnp.float32
    )
    numer = numer + diagonal_portion.reshape(per_dev * BLOCK_TOKENS, HEAD_SIZE)
    return (numer / total).astype(jnp.bfloat16)


def shards(
    queries, key_rows, value_rows, slash_offsets, union_blocks, head_picks, owner_counts, out_weight
):
    tokens = queries.shape[0]
    per_dev = tokens // BLOCK_TOKENS
    heads_here = slash_offsets.shape[0]
    groups_here = key_rows.shape[1] // HEAD_SIZE
    group_size = heads_here // groups_here
    owners = lax.axis_size("ctx")
    device_rank = lax.axis_index("ctx")
    scale_of_scores = jnp.float32(HEAD_SIZE ** (-0.5))
    stacked = jnp.stack([key_rows, value_rows])
    previous = from_behind(stacked, "ctx", 1)
    extended = jnp.concatenate([previous, stacked], axis=1).reshape(
        2, 2 * per_dev, BLOCK_TOKENS, groups_here, HEAD_SIZE
    )
    local_blocks = stacked.reshape(2, per_dev, BLOCK_TOKENS, groups_here, HEAD_SIZE)
    head_group = jnp.arange(heads_here, dtype=jnp.int32) // group_size
    mine_union = lax.dynamic_index_in_dim(union_blocks, device_rank, 1, keepdims=False)
    owner_base = jnp.arange(owners, dtype=jnp.int32)[:, None] * per_dev
    slot_rank = jnp.arange(VPER, dtype=jnp.int32)
    chosen = slot_rank[None, None, :] < owner_counts[:, :, None]
    mine_picks = lax.dynamic_index_in_dim(head_picks, device_rank, 1, keepdims=False)
    chosen_local = jnp.take_along_axis(mine_union[head_group], mine_picks, axis=1)
    block_rows = local_blocks[:, chosen_local, :, head_group[:, None], :]
    gathered = lax.all_gather(block_rows[:, None], "ctx", axis=1, tiled=True)
    slot_block = owner_base[None] + jnp.take_along_axis(
        union_blocks[head_group], head_picks, axis=2
    )
    source_of = list(range(heads_here))
    query_place = device_rank * tokens + jnp.arange(tokens, dtype=jnp.int32)
    query_block = device_rank * per_dev + jnp.arange(per_dev, dtype=jnp.int32)
    inner_offset = jnp.arange(BLOCK_TOKENS, dtype=jnp.int32)
    local_index = jnp.arange(per_dev, dtype=jnp.int32)
    per_head = []
    for head_index in range(heads_here):
        kv_index = head_index // group_size
        offsets = slash_offsets[head_index]
        query_head = queries[:, head_index * HEAD_SIZE : (head_index + 1) * HEAD_SIZE]
        vertical = gathered[source_of[head_index]]
        blocks_flat = slot_block[head_index].reshape(-1)
        valid_flat = chosen[head_index].reshape(-1)
        slot_count = blocks_flat.shape[0]
        vert_keys = vertical[:, :, 0].reshape(slot_count * BLOCK_TOKENS, HEAD_SIZE)
        vert_values = vertical[:, :, 1].reshape(slot_count * BLOCK_TOKENS, HEAD_SIZE)
        vert_scores = (
            jnp.einsum("qd,kd->qk", query_head, vert_keys, preferred_element_type=jnp.float32)
            * scale_of_scores
        )
        distance = query_block[:, None] - blocks_flat[None, :]
        on_slash = jnp.any(distance[:, :, None] == offsets[None, None, :], axis=2)
        block_mask = valid_flat[None, :] & jnp.logical_not(on_slash)
        key_place = (blocks_flat[:, None] * BLOCK_TOKENS + inner_offset[None, :]).reshape(-1)
        vert_mask = jnp.broadcast_to(
            block_mask[:, None, :, None], (per_dev, BLOCK_TOKENS, slot_count, BLOCK_TOKENS)
        ).reshape(tokens, slot_count * BLOCK_TOKENS)
        vert_mask = vert_mask & (key_place[None, :] <= query_place[:, None])
        group_slab = extended[:, :, :, kv_index, :]
        ext_index = local_index[:, None] + per_dev - offsets[None, :]
        slash_rows = group_slab[:, ext_index]
        diagonal_scores = (
            jnp.einsum(
                "hax,hisx->hais",
                query_head.reshape(per_dev, BLOCK_TOKENS, HEAD_SIZE),
                slash_rows[0],
                preferred_element_type=jnp.float32,
            )
            * scale_of_scores
        )
        slash_valid = query_block[:, None] - offsets[None, :] >= 0
        slash_mask = slash_valid[:, None, :, None] & (
            (offsets[None, None, :, None] > 0)
            | (inner_offset[None, None, None, :] <= inner_offset[None, :, None, None])
        )
        slash_mask = slash_mask.reshape(tokens, NS * BLOCK_TOKENS)
        per_head.append(
            attend(
                vert_scores,
                vert_mask,
                diagonal_scores.reshape(tokens, NS * BLOCK_TOKENS),
                slash_mask,
                vert_values,
                slash_rows[1],
                per_dev,
            )
        )
    attended = jnp.concatenate(per_head, axis=1)
    projected = jnp.dot(
        lax.all_gather(attended, "head", axis=1, tiled=True),
        out_weight,
        preferred_element_type=jnp.float32,
    )
    return projected.astype(jnp.bfloat16)


def solution(mesh):
    in_specs = (
        P("ctx", "head"),
        P("ctx", "head"),
        P("ctx", "head"),
        P("head", None),
        P("head", None, None),
        P("head", None, None),
        P("head", None),
        P(None, "head"),
    )
    out_specs = P("ctx", "head")
    return jax.shard_map(shards, mesh=mesh, in_specs=in_specs, out_specs=out_specs, check_vma=False)
```

profile of v0, /device:TPU:1, one launch (start us, length us, event | category | flops | bytes accessed | tf_op | source)
XLA Modules:
  0.0 189.1 jit_solution(1846127941252690670)
XLA Ops:
  6.5 0.8 constant_dynamic-slice_fusion
  7.5 0.9 dynamic-slice_reduce_fusion
  9.1 1.0 pad_maximum_fusion.1
  10.1 1.2 gather_fusion
  11.4 1.0 pad_maximum_fusion.2
  12.4 4.4 %collective-permute-start = (bf16[2,512,128]{2,1,0:T(8,128)(2,1)S(1)}, bf16[2,512,128]{2,1,0:T(8,128)(2,1)S(1)}, u32[]{:S(2)}, u32[]{:S(2)}) collective-permute-start(bf16[2,512,128]{2,1,0:T(8,128)(2,1)S(1)} %pad_maximum_fusion.2), channel_id=1, source_target_pairs={{0,8},{8,16},{16,24},{24,32},{32,40},{40,48},{48,56},{56,64},{64,7... | collective-permute-start | bytes 786440 | tf_op jit(solution)/shard_map/ppermute | solution.py:15
  16.8 0.7 fusion.89
  17.6 0.8 copy.55
  18.3 1.5 gather_fusion.5
  21.6 0.8 broadcast_or_fusion.3
  23.7 4.7 %reshape.1051 = pred[512,2048]{0,1:T(32,128)(4,1)} reshape(pred[8,64,32,64]{1,0,3,2:T(8,128)(4,1)S(1)} %broadcast_in_dim.29) | data formatting | bytes 2097152 | tf_op jit(solution)/shard_map/reshape | solution.py:98
  29.8 4.7 %reshape.1054 = pred[512,2048]{0,1:T(32,128)(4,1)} reshape(pred[8,64,32,64]{1,0,3,2:T(8,128)(4,1)S(1)} %broadcast_in_dim.33) | data formatting | bytes 2097152 | tf_op jit(solution)/shard_map/reshape | solution.py:98
  35.9 4.7 %reshape.1057 = pred[512,2048]{0,1:T(32,128)(4,1)} reshape(pred[8,64,32,64]{1,0,3,2:T(8,128)(4,1)S(1)} %broadcast_in_dim.34) | data formatting | bytes 2097152 | tf_op jit(solution)/shard_map/reshape | solution.py:98
  42.0 4.7 %reshape.1060 = pred[512,2048]{0,1:T(32,128)(4,1)} reshape(pred[8,64,32,64]{1,0,3,2:T(8,128)(4,1)S(1)} %broadcast_in_dim.35) | data formatting | bytes 2097152 | tf_op jit(solution)/shard_map/reshape | solution.py:98
  47.4 0.7 fusion.99
  48.2 0.7 gather_fusion.1
  49.1 1.0 copy-done.9
  50.0 1.3 fusion.107
  51.5 0.7 gather_fusion.2
  52.3 1.0 copy-done.8
  54.4 0.7 gather_fusion.3
  55.2 1.0 copy-done.7
  57.2 1.7 gather_fusion.4
  58.9 1.3 copy.70
  60.2 1.0 copy-done.5
  61.6 32.7 %all-gather.6.cloned.1.call-done = bf16[4,64,64,128]{3,2,1,0:T(8,128)(2,1)} async-done(((bf16[4,2,64,128]{3,2,1,0:T(8,128)(2,1)}), bf16[4,64,64,128]{3,2,1,0:T(8,128)(2,1)}) %all-gather.6.cloned.1.call-update) | async-done | bytes 4194320 | tf_op jit(solution)/shard_map/all_gather | solution.py:68
  94.4 4.4 %fusion.94 = (bf16[1,64,64,128]{3,2,1,0:T(8,128)(2,1)S(1)}, bf16[1,64,64,128]{3,2,1,0:T(8,128)(2,1)}, bf16[1,64,64,128]{3,2,1,0:T(8,128)(2,1)}, bf16[1,64,64,128]{3,2,1,0:T(8,128)(2,1)}) fusion(bf16[4,64,64,128]{3,2,1,0:T(8,128)(2,1)} %all-gather.6.cloned.1.call-done), kind=kLoop, calls=%fused_computation.176 | loop fusion | bytes 8388608 | tf_op jit(solution)/shard_map/slice | solution.py:82
  98.8 0.9 fusion.95
  99.7 3.6 %fusion.106 = (f32[512]{0:T(512)S(1)}, f32[512,2048]{0,1:T(8,128)}) fusion(bf16[2048,128]{1,0:T(8,128)(2,1)S(1)} %bitcast.252, bf16[512,512]{1,0:T(8,128)(2,1)} %param.8, pred[512,2048]{0,1:T(32,128)(4,1)S(1)} %copy-done.19, s32[512]{0:T(512)S(1)} %copy-done.37, s32[2048]{0:T(1024)S(1)} %copy-done.32), kind=kOutput, calls=%fused_computation.188 | convolution fusion | flops 273677824 | bytes 5910528 | tf_op jit(solution)/shard_map/qd,kd->qk/dot_general | solution.py:89
  103.3 1.5 fusion.64
  104.8 1.7 fusion.78
  106.5 2.1 %fusion.96 = (bf16[32,1,1,64,128]{4,3,2,0,1:T(8,128)(2,1)}, bf16[32,1,1,64,128]{4,3,2,0,1:T(8,128)(2,1)S(1)}) fusion(bf16[32,1,2,64,128]{4,3,2,0,1:T(8,128)(2,1)} %bitcast.227), kind=kLoop, calls=%fused_computation.178 | loop fusion | bytes 2097152 | tf_op jit(solution)/shard_map/slice | solution.py:87
  108.6 3.6 %fusion.104 = (f32[512]{0:T(512)S(1)}, f32[512,2048]{0,1:T(8,128)}) fusion(bf16[2048,128]{1,0:T(8,128)(2,1)S(1)} %bitcast.253, bf16[512,512]{1,0:T(8,128)(2,1)} %param.8, pred[512,2048]{0,1:T(32,128)(4,1)S(1)} %copy-done.18, s32[512]{0:T(512)S(1)} %copy-done.37, s32[2048]{0:T(1024)S(1)} %copy-done.31), kind=kOutput, calls=%fused_computation.186 | convolution fusion | flops 273677824 | bytes 5910528 | tf_op jit(solution)/shard_map/qd,kd->qk/dot_general | solution.py:89
  112.5 2.2 %fusion.76 = f32[8,64,128,1]{2,1,3,0:T(8,128)} fusion(f32[8,64,4,64]{1,3,2,0:T(8,128)S(1)} %get-tuple-element.68, bf16[2,8,4,64,128]{4,3,2,1,0:T(8,128)(2,1)} %bitcast.234, f32[8,64]{1,0:T(8,128)S(1)} %max.47), kind=kOutput, calls=%fused_computation.70 | convolution fusion | flops 33816576 | bytes 1312768 | tf_op jit(solution)/shard_map/wojf,wjfl->wol/dot_general | solution.py:36
  114.7 2.1 %fusion.97 = (bf16[32,1,1,64,128]{4,3,2,0,1:T(8,128)(2,1)}, bf16[32,1,1,64,128]{4,3,2,0,1:T(8,128)(2,1)S(1)}) fusion(bf16[32,1,2,64,128]{4,3,2,0,1:T(8,128)(2,1)} %bitcast.226), kind=kLoop, calls=%fused_computation.179 | loop fusion | bytes 2097152 | tf_op jit(solution)/shard_map/slice | solution.py:87
  116.8 3.7 %fusion.102 = (f32[512]{0:T(512)S(1)}, f32[512,2048]{0,1:T(8,128)}) fusion(bf16[2048,128]{1,0:T(8,128)(2,1)S(1)} %bitcast.254, bf16[512,512]{1,0:T(8,128)(2,1)} %param.8, pred[512,2048]{0,1:T(32,128)(4,1)S(1)} %copy-done.17, s32[512]{0:T(512)S(1)} %copy-done.37, s32[2048]{0:T(1024)S(1)} %copy-done.30), kind=kOutput, calls=%fused_computation.184 | convolution fusion | flops 273677824 | bytes 5910528 | tf_op jit(solution)/shard_map/qd,kd->qk/dot_general | solution.py:89
  120.8 2.2 %fusion.74 = f32[8,64,128,1]{2,1,3,0:T(8,128)} fusion(f32[8,64,4,64]{1,3,2,0:T(8,128)S(1)} %get-tuple-element.64, bf16[2,8,4,64,128]{4,3,2,1,0:T(8,128)(2,1)} %bitcast.232, f32[8,64]{1,0:T(8,128)S(1)} %max.49), kind=kOutput, calls=%fused_computation.69 | convolution fusion | flops 33816576 | bytes 1312768 | tf_op jit(solution)/shard_map/wojf,wjfl->wol/dot_general | solution.py:36
  123.0 0.9 fusion.98
  123.9 3.7 %fusion.100 = (f32[512]{0:T(512)S(1)}, f32[512,2048]{0,1:T(8,128)}) fusion(bf16[2048,128]{1,0:T(8,128)(2,1)S(1)} %bitcast.251, bf16[512,512]{1,0:T(8,128)(2,1)} %param.8, pred[512,2048]{0,1:T(32,128)(4,1)S(1)} %copy-done.16, s32[512]{0:T(512)S(1)} %copy-done.37, s32[2048]{0:T(1024)S(1)} %copy-done.29), kind=kOutput, calls=%fused_computation.182 | convolution fusion | flops 273677824 | bytes 5910528 | tf_op jit(solution)/shard_map/qd,kd->qk/dot_general | solution.py:89
  129.1 3.0 %fusion = f32[512]{0:T(512)S(1)} fusion(f32[512,2048]{0,1:T(8,128)} %get-tuple-element.70, f32[512]{0:T(512)S(1)} %max.44), kind=kLoop, calls=%fused_computation.15 | loop fusion | flops 2096640 | bytes 4198400 | tf_op jit(solution)/shard_map/reduce_sum | solution.py:28
  134.5 0.8 copy-done.3
  136.5 0.8 fusion.61
  137.3 0.7 fusion.58
  138.1 0.8 fusion.55
  138.8 0.8 fusion.52
  139.6 0.8 pad_maximum_fusion
  140.5 35.2 %all-gather.4.cloned.1.call-done = bf16[512,4096]{0,1:T(8,128)(2,1)} async-done(((bf16[512,512]{0,1:T(8,128)(2,1)}), bf16[512,4096]{0,1:T(8,128)(2,1)}) %all-gather.4.cloned.1.call-update) | async-done | bytes 4194320 | tf_op jit(solution)/shard_map/all_gather | solution.py:131
  175.7 6.6 %convolution_convert_fusion = bf16[512,512]{1,0:T(8,128)(2,1)} fusion(bf16[512,4096]{0,1:T(8,128)(2,1)} %all-gather.4.cloned.1.call-done, bf16[4096,512]{1,0:T(8,128)(2,1)} %param.15), kind=kOutput, calls=%fused_computation.43 | convolution fusion | flops 2147745792 | bytes 8912896 | tf_op jit(solution)/shard_map/dot_general | solution.py:130
  (186 shorter events, 17.3 us)
Async XLA Ops:
  6.5 13.9 %copy-start.28 = (s32[4,32,1]{1,2,0:T(1,128)S(1)}, s32[4,32,1]{1,2,0:T(1,128)}, u32[]{:S(2)}) copy-start(s32[4,32,1]{1,2,0:T(1,128)} %param.13) | copy-start | bytes 1540
  6.5 13.4 %copy-start.35 = (s32[4,4]{1,0:T(4,128)S(1)}, s32[4,4]{1,0:T(4,128)}, u32[]{:S(2)}) copy-start(s32[4,4]{1,0:T(4,128)} %param.11) | copy-start | bytes 196
  6.5 14.2 %copy-start.36 = (s32[4,32]{1,0:T(4,128)S(1)}, s32[4,32]{1,0:T(4,128)}, u32[]{:S(2)}) copy-start(s32[4,32]{1,0:T(4,128)} %param.14) | copy-start | bytes 1540
  6.5 87.9 %all-gather.6.cloned.1.call-start = ((), (), s32[]{:S(2)}) async-start(), calls=%async_computation.1 | async-start | bytes 4325376 | tf_op jit(solution)/shard_map/all_gather | solution.py:68
  11.3 164.4 %all-gather.4.cloned.1.call-start = ((), (), s32[]{:S(2)}) async-start(), calls=%async_computation | async-start | bytes 4718592 | tf_op jit(solution)/shard_map/all_gather | solution.py:131
  12.4 35.8 %collective-permute-start = (bf16[2,512,128]{2,1,0:T(8,128)(2,1)S(1)}, bf16[2,512,128]{2,1,0:T(8,128)(2,1)S(1)}, u32[]{:S(2)}, u32[]{:S(2)}) collective-permute-start(bf16[2,512,128]{2,1,0:T(8,128)(2,1)S(1)} %pad_maximum_fusion.2), channel_id=1, source_target_pairs={{0,8},{8,16},{16,24},{24,32},{32,40},{40,48},{48,56},{56,64},{64,7... | collective-permute-start | bytes 786440 | tf_op jit(solution)/shard_map/ppermute | solution.py:15
  35.9 11.5 %copy-start.22 = (bf16[512,512]{1,0:T(8,128)(2,1)S(1)}, bf16[512,512]{1,0:T(8,128)(2,1)}, u32[]{:S(2)}) copy-start(bf16[512,512]{1,0:T(8,128)(2,1)} %param.8) | copy-start | bytes 1572868
  35.9 12.2 %copy-start.14 = (bf16[512,128]{1,0:T(8,128)(2,1)S(1)}, bf16[512,128]{1,0:T(8,128)(2,1)}, u32[]{:S(2)}) copy-start(bf16[512,128]{1,0:T(8,128)(2,1)} %param.10) | copy-start | bytes 393220
  35.9 12.2 %copy-start.15 = (bf16[512,128]{1,0:T(8,128)(2,1)S(1)}, bf16[512,128]{1,0:T(8,128)(2,1)}, u32[]{:S(2)}) copy-start(bf16[512,128]{1,0:T(8,128)(2,1)} %param.9) | copy-start | bytes 393220
  46.7 3.3 %copy-start.27 = (pred[64,4,64]{0,2,1:T(8,128)(4,1)S(1)}, pred[64,4,64]{0,2,1:T(8,128)(4,1)}, u32[]{:S(2)}) copy-start(pred[64,4,64]{0,2,1:T(8,128)(4,1)} %get-tuple-element.21) | copy-start | bytes 49156
  46.7 3.3 %copy-start.41 = (pred[8,4]{1,0:T(8,128)(4,1)S(1)}, pred[8,4]{1,0:T(8,128)(4,1)}, u32[]{:S(2)}) copy-start(pred[8,4]{1,0:T(8,128)(4,1)} %get-tuple-element.49) | copy-start | bytes 100
  49.0 4.4 %copy-start.26 = (pred[64,4,64]{0,2,1:T(8,128)(4,1)S(1)}, pred[64,4,64]{0,2,1:T(8,128)(4,1)}, u32[]{:S(2)}) copy-start(pred[64,4,64]{0,2,1:T(8,128)(4,1)} %get-tuple-element.22) | copy-start | bytes 49156
  49.0 4.4 %copy-start.40 = (pred[8,4]{1,0:T(8,128)(4,1)S(1)}, pred[8,4]{1,0:T(8,128)(4,1)}, u32[]{:S(2)}) copy-start(pred[8,4]{1,0:T(8,128)(4,1)} %get-tuple-element.50) | copy-start | bytes 100
  49.1 1.0 copy-start.9
  52.2 4.0 %copy-start.23 = (bf16[512,128]{1,0:T(8,128)(2,1)S(1)}, bf16[512,128]{1,0:T(8,128)(2,1)}, u32[]{:S(2)}) copy-start(bf16[512,128]{1,0:T(8,128)(2,1)} %get-tuple-element.20) | copy-start | bytes 393220
  52.2 4.0 %copy-start.25 = (pred[64,4,64]{0,2,1:T(8,128)(4,1)S(1)}, pred[64,4,64]{0,2,1:T(8,128)(4,1)}, u32[]{:S(2)}) copy-start(pred[64,4,64]{0,2,1:T(8,128)(4,1)} %get-tuple-element.23) | copy-start | bytes 49156
  52.2 4.0 %copy-start.39 = (pred[8,4]{1,0:T(8,128)(4,1)S(1)}, pred[8,4]{1,0:T(8,128)(4,1)}, u32[]{:S(2)}) copy-start(pred[8,4]{1,0:T(8,128)(4,1)} %get-tuple-element.51) | copy-start | bytes 100
  52.3 1.0 copy-start.8
  55.1 6.1 %copy-start.24 = (pred[64,4,64]{0,2,1:T(8,128)(4,1)S(1)}, pred[64,4,64]{0,2,1:T(8,128)(4,1)}, u32[]{:S(2)}) copy-start(pred[64,4,64]{0,2,1:T(8,128)(4,1)} %get-tuple-element.24) | copy-start | bytes 49156
  55.1 6.1 %copy-start.38 = (pred[8,4]{1,0:T(8,128)(4,1)S(1)}, pred[8,4]{1,0:T(8,128)(4,1)}, u32[]{:S(2)}) copy-start(pred[8,4]{1,0:T(8,128)(4,1)} %get-tuple-element.52) | copy-start | bytes 100
  55.2 1.0 copy-start.7
  60.2 1.0 copy-start.5
  61.6 38.0 %copy-start.32 = (s32[2048]{0:T(1024)S(1)}, s32[2048]{0:T(1024)}, u32[]{:S(2)}) copy-start(s32[2048]{0:T(1024)} %add.293) | copy-start | bytes 24580
  61.6 38.0 %copy-start.37 = (s32[512]{0:T(512)S(1)}, s32[512]{0:T(512)}, u32[]{:S(2)}) copy-start(s32[512]{0:T(512)} %iota_add_fusion.4) | copy-start | bytes 6148
  94.4 5.3 %copy-start.19 = (pred[512,2048]{0,1:T(32,128)(4,1)S(1)}, pred[512,2048]{0,1:T(32,128)(4,1)}, u32[]{:S(2)}) copy-start(pred[512,2048]{0,1:T(32,128)(4,1)} %reshape.1051) | copy-start | bytes 3145732
  99.7 8.9 %copy-start.31 = (s32[2048]{0:T(1024)S(1)}, s32[2048]{0:T(1024)}, u32[]{:S(2)}) copy-start(s32[2048]{0:T(1024)} %add.307) | copy-start | bytes 24580
  103.3 5.3 %copy-start.18 = (pred[512,2048]{0,1:T(32,128)(4,1)S(1)}, pred[512,2048]{0,1:T(32,128)(4,1)}, u32[]{:S(2)}) copy-start(pred[512,2048]{0,1:T(32,128)(4,1)} %reshape.1054) | copy-start | bytes 3145732
  108.6 8.2 %copy-start.30 = (s32[2048]{0:T(1024)S(1)}, s32[2048]{0:T(1024)}, u32[]{:S(2)}) copy-start(s32[2048]{0:T(1024)} %add.314) | copy-start | bytes 24580
  112.3 4.5 %copy-start.17 = (pred[512,2048]{0,1:T(32,128)(4,1)S(1)}, pred[512,2048]{0,1:T(32,128)(4,1)}, u32[]{:S(2)}) copy-start(pred[512,2048]{0,1:T(32,128)(4,1)} %reshape.1057) | copy-start | bytes 3145732
  116.8 6.2 %copy-start.4 = (bf16[1,64,64,128]{3,2,1,0:T(8,128)(2,1)S(1)}, bf16[1,64,64,128]{3,2,1,0:T(8,128)(2,1)}, u32[]{:S(2)}) copy-start(bf16[1,64,64,128]{3,2,1,0:T(8,128)(2,1)} %get-tuple-element.8) | copy-start | bytes 3145732
  116.8 7.0 %copy-start.29 = (s32[2048]{0:T(1024)S(1)}, s32[2048]{0:T(1024)}, u32[]{:S(2)}) copy-start(s32[2048]{0:T(1024)} %add.321) | copy-start | bytes 24580
  120.6 3.3 %copy-start.16 = (pred[512,2048]{0,1:T(32,128)(4,1)S(1)}, pred[512,2048]{0,1:T(32,128)(4,1)}, u32[]{:S(2)}) copy-start(pred[512,2048]{0,1:T(32,128)(4,1)} %reshape.1060) | copy-start | bytes 3145732
  123.8 4.0 %copy-start.6 = (bf16[32,2,64,128]{3,2,0,1:T(8,128)(2,1)S(1)}, bf16[32,2,64,128]{3,2,0,1:T(8,128)(2,1)}, u32[]{:S(2)}) copy-start(bf16[32,2,64,128]{3,2,0,1:T(8,128)(2,1)} %copy-done.5) | copy-start | bytes 3145732
  123.8 4.6 %copy-start.33 = (f32[512]{0:T(512)S(1)}, f32[512]{0:T(512)}, u32[]{:S(2)}) copy-start(f32[512]{0:T(512)} %reduce_max.94) | copy-start | bytes 6148
  123.8 4.7 %copy-start.20 = (f32[8,64,128,1]{2,1,3,0:T(8,128)S(1)}, f32[8,64,128,1]{2,1,3,0:T(8,128)}, u32[]{:S(2)}) copy-start(f32[8,64,128,1]{2,1,3,0:T(8,128)} %fusion.76) | copy-start | bytes 786436
  123.9 4.8 %copy-start.34 = (f32[512]{0:T(512)S(1)}, f32[512]{0:T(512)}, u32[]{:S(2)}) copy-start(f32[512]{0:T(512)} %reduce_max.98) | copy-start | bytes 6148
  123.9 4.9 %copy-start.21 = (f32[8,64,128,1]{2,1,3,0:T(8,128)S(1)}, f32[8,64,128,1]{2,1,3,0:T(8,128)}, u32[]{:S(2)}) copy-start(f32[8,64,128,1]{2,1,3,0:T(8,128)} %fusion.74) | copy-start | bytes 786436
  129.0 6.9 %copy-start.10 = (bf16[32,1,1,64,128]{4,3,2,0,1:T(8,128)(2,1)S(1)}, bf16[32,1,1,64,128]{4,3,2,0,1:T(8,128)(2,1)}, u32[]{:S(2)}) copy-start(bf16[32,1,1,64,128]{4,3,2,0,1:T(8,128)(2,1)} %get-tuple-element.9) | copy-start | bytes 1572868
  129.1 3.5 %copy-start.1 = (f32[512,2048]{0,1:T(8,128)S(1)}, f32[512,2048]{0,1:T(8,128)}, u32[]{:S(2)}) copy-start(f32[512,2048]{0,1:T(8,128)} %get-tuple-element.66) | copy-start | bytes 12582916
  129.1 4.7 %copy-start.2 = (f32[512,2048]{0,1:T(8,128)S(1)}, f32[512,2048]{0,1:T(8,128)}, u32[]{:S(2)}) copy-start(f32[512,2048]{0,1:T(8,128)} %get-tuple-element.62) | copy-start | bytes 12582916
  132.6 2.7 %copy-start.3 = (f32[512,2048]{0,1:T(8,128)S(1)}, f32[512,2048]{0,1:T(8,128)}, u32[]{:S(2)}) copy-start(f32[512,2048]{0,1:T(8,128)} %get-tuple-element.58) | copy-start | bytes 12582916
  133.8 2.7 %copy-start = (f32[512,2048]{0,1:T(8,128)S(1)}, f32[512,2048]{0,1:T(8,128)}, u32[]{:S(2)}) copy-start(f32[512,2048]{0,1:T(8,128)} %get-tuple-element.70) | copy-start | bytes 12582916
  135.3 2.0 %copy-start.11 = (bf16[32,1,1,64,128]{4,3,2,0,1:T(8,128)(2,1)S(1)}, bf16[32,1,1,64,128]{4,3,2,0,1:T(8,128)(2,1)}, u32[]{:S(2)}) copy-start(bf16[32,1,1,64,128]{4,3,2,0,1:T(8,128)(2,1)} %get-tuple-element.11) | copy-start | bytes 1572868
  136.5 1.5 copy-start.12
  137.3 1.5 copy-start.13
Sparse Core Ops, SparseCore 0:
  11.4 82.9 all-gather.5
  140.6 35.0 all-gather.3
where the time goes:
time: 190 us; the launch traced here: 189 us
  waiting for transfers between devices  68 us (36%)
  local copies, waits for them, and re-layouts  56.4 us (30%)
  matrix products  33 us (17%)
  between operations  14.1 us (7%)
  other arithmetic  13.2 us (7%)
  starting transfers between devices  4.43 us (2%)
    all_gather x1, waiting for transfers between devices, shards(): lax.all_gather(attended, 'head', axis=1, tiled=True)  35.2 us
    all_gather x1, waiting for transfers between devices, shards(): gathered = lax.all_gather(block_rows[:, None], 'ctx', axis=1, tiled=True)  32.7 us
    reshape x4, local copies, waits for them, and re-layouts, shards(): vert_mask = jnp.broadcast_to(block_mask[:, None, :, None], (per_dev, BLOC...  18.9 us
    dot_general x4, matrix products, shards(): jnp.einsum('qd,kd->qk', query_head, vert_keys, preferred_element_type=jnp...  14.6 us
    unnamed x88, local copies, waits for them, and re-layouts  6.68 us
    dot_general x1, matrix products, shards(): jnp.dot(lax.all_gather(attended, 'head', axis=1, tiled=True), out_weight,...  6.61 us
    dot_general x4, matrix products, attend(): jnp.einsum('wojf,wjfl->wol', slash_probability, diagonal_values, preferre...  6.35 us
    slice x4, local copies, waits for them, and re-layouts, shards(): vertical[:, :, 1].reshape(slot_count * BLOCK_TOKENS, HEAD_SIZE)  5.9 us
  transfers between devices with their start and end apart: 3, of which 2 were waited for; matrix products, arithmetic and copies ran while one was open for 22% of the time, Pallas kernels for 0%

commit v1 on v0

v1 whole, which is shorter than its diff:
```python
import functools

import jax
import jax.numpy as jnp
from jax import lax
from jax.experimental import pallas as pl
from jax.experimental.pallas import tpu as pltpu
from jax.sharding import PartitionSpec as P

HEAD_SIZE = 128
BLOCK = 64
NS = 4
HEADS = 4
OWNERS = 32
PER_DEV = 8
TOKENS = 512
NX, NZ, NY = 4, 8, 4
TILE = 256
NEAR = 6 * BLOCK
NEG = -1e30
SCALE = HEAD_SIZE**-0.5
MESH = pl.DeviceIdType.MESH


def kernel(
    slash, union, picks, counts, q_hbm, k_hbm, v_hbm, w_hbm, out_ref,
    q_ref, k_own, v_own, ke, ve, w_ref, pieces, kh, vh, scores, near_scores, near_probs, numer, att, acc,
    far_bias, local_sem, send_sem, recv_sem, ysend_sem, yrecv_sem,
):
    c = lax.axis_index("ctx")
    hd = lax.axis_index("head")
    x, z = c // NZ, lax.rem(c, NZ)
    y, core = hd // 2, lax.rem(hd, 2)

    def at_xz(dx, dz):
        return {"ctx": lax.rem(x + dx + NX, NX) * NZ + lax.rem(z + dz + NZ, NZ)}

    def at_y(dy):
        return {"head": lax.rem(y + dy + NY, NY) * 2 + core}

    sibling = {"head": y * 2 + 1 - core}
    after = {"ctx": lax.rem(c + 1, OWNERS)}
    before = {"ctx": lax.rem(c + OWNERS - 1, OWNERS)}

    k_in = pltpu.make_async_copy(k_hbm, ke.at[pl.ds(PER_DEV, PER_DEV)], local_sem.at[0])
    v_in = pltpu.make_async_copy(v_hbm, ve.at[pl.ds(PER_DEV, PER_DEV)], local_sem.at[1])
    q_in = pltpu.make_async_copy(q_hbm, q_ref, local_sem.at[2])
    w_in = pltpu.make_async_copy(w_hbm, w_ref, local_sem.at[3])
    k_pack = pltpu.make_async_copy(k_hbm, k_own, local_sem.at[4])
    v_pack = pltpu.make_async_copy(v_hbm, v_own, local_sem.at[5])
    for copy in (k_pack, v_pack, k_in, v_in, q_in, w_in):
        copy.start()

    barrier = pltpu.get_barrier_semaphore()
    peers = (
        at_xz(1, 0), at_xz(-1, 0), at_xz(0, 1), at_xz(0, -1), after, before,
        sibling, at_y(1), at_y(-1),
    )
    for peer in peers:
        pl.semaphore_signal(barrier, inc=1, device_id=peer, device_id_type=MESH)

    vh[:, HEAD_SIZE:] = jnp.ones((OWNERS * BLOCK, HEAD_SIZE), jnp.bfloat16)
    acc[...] = jnp.zeros_like(acc)

    k_pack.wait()
    v_pack.wait()
    own = (z * 8 + x * 2, 64 + x * 16 + z * 2)
    for u in range(2):
        pieces[own[u]] = k_own[union[0, u, c]]
        pieces[own[u] + 1] = v_own[union[0, u, c]]

    def remote(ref, at, size, sem, device):
        part = ref.at[pl.ds(at, size)]
        return pltpu.make_async_remote_copy(
            src_ref=part, dst_ref=part, send_sem=send_sem.at[sem], recv_sem=recv_sem.at[sem],
            device_id=device, device_id_type=MESH,
        )

    def xs(d):
        return lax.rem(x + d + 2 * NX, NX)

    def zs(d):
        return lax.rem(z + d + 2 * NZ, NZ)

    def a1(step, way, d):
        half = 0 if step == 1 else (0 if way > 0 else 1)
        size = 2 if step == 1 else 1
        sem = (step - 1) * 2 + (0 if way > 0 else 1)
        dev = at_xz(way, 0)
        return remote(pieces, z * 8 + xs(-way * d) * 2 + half, size, sem, dev)

    def b1(step, way, d):
        half = 0 if step < 4 else (0 if way > 0 else 1)
        size = 2 if step < 4 else 1
        sem = 4 + (step - 1) * 2 + (0 if way > 0 else 1)
        dev = at_xz(0, way)
        return remote(pieces, 64 + x * 16 + zs(-way * d) * 2 + half, size, sem, dev)

    def a2(step, way, d):
        half = 0 if step < 4 else (0 if way > 0 else 4)
        size = 8 if step < 4 else 4
        sem = 12 + (step - 1) * 2 + (0 if way > 0 else 1)
        dev = at_xz(0, way)
        return remote(pieces, zs(-way * d) * 8 + half, size, sem, dev)

    def b2(step, way, d):
        half = 0 if step == 1 else (0 if way > 0 else 8)
        size = 16 if step == 1 else 8
        sem = 20 + (step - 1) * 2 + (0 if way > 0 else 1)
        dev = at_xz(way, 0)
        return remote(pieces, 64 + xs(-way * d) * 16 + half, size, sem, dev)

    def previous(ref, sem):
        return pltpu.make_async_remote_copy(
            src_ref=ref.at[pl.ds(PER_DEV, PER_DEV)], dst_ref=ref.at[pl.ds(0, PER_DEV)],
            send_sem=send_sem.at[sem], recv_sem=recv_sem.at[sem],
            device_id=after, device_id_type=MESH,
        )

    pl.semaphore_wait(barrier, len(peers))

    def go(kind, step):
        for way in (1, -1):
            kind(step, way, step - 1).start()

    def come(kind, step):
        for way in (1, -1):
            kind(step, way, step).wait_recv()

    go(a1, 1)
    go(b1, 1)
    come(a1, 1)
    go(a1, 2)
    come(b1, 1)
    go(b1, 2)
    come(a1, 2)
    go(a2, 1)
    come(b1, 2)
    go(b1, 3)
    k_in.wait()
    v_in.wait()
    previous(ke, 24).start()
    previous(ve, 25).start()

    for j in range(HEADS):
        for o in range(OWNERS):
            seen = jnp.logical_and(counts[j, o] > 0, o <= c - 2)
            value = jnp.where(seen, 0.0, NEG).astype(jnp.float32)
            far_bias[j, :, o * BLOCK : (o + 1) * BLOCK] = jnp.full((8, BLOCK), value, jnp.float32)

    come(b1, 3)
    go(b1, 4)
    come(a2, 1)
    go(a2, 2)
    come(b1, 4)
    go(b2, 1)
    come(a2, 2)
    go(a2, 3)
    come(b2, 1)
    go(b2, 2)
    come(a2, 3)
    go(a2, 4)
    q_in.wait()
    previous(ke, 24).wait_recv()
    previous(ve, 25).wait_recv()
    come(b2, 2)
    come(a2, 4)

    lane = lax.broadcasted_iota(jnp.int32, (BLOCK, 2 * BLOCK), 1)
    row = lax.broadcasted_iota(jnp.int32, (BLOCK, 2 * BLOCK), 0)
    low = lane < BLOCK
    causal = jnp.where((lane % BLOCK) <= row, 0.0, NEG).astype(jnp.float32)
    c_before = jnp.maximum(c - 1, 0)
    ones = jnp.ones((NEAR, HEAD_SIZE), jnp.bfloat16)

    def picked(j, owner):
        first, second = union[0, 0, owner], union[0, 1, owner]
        return first + picks[j, 0, owner] * (second - first)

    def near_blocks(j, i):
        slashes = [i + PER_DEV - slash[j, s] for s in range(NS)]
        return slashes + [picked(j, c_before), PER_DEV + picked(j, c)]

    def attend(j):
        columns = pl.ds(pl.multiple_of(j * HEAD_SIZE, HEAD_SIZE), HEAD_SIZE)
        for o in range(OWNERS):
            first, second = (o % NZ) * 8 + (o // NZ) * 2, 64 + 2 * o
            at = first + picks[j, 0, o] * (second - first)
            kh[o * BLOCK : (o + 1) * BLOCK, :] = pieces[at]
            vh[o * BLOCK : (o + 1) * BLOCK, :HEAD_SIZE] = pieces[at + 1]

        def near(i, _):
            rows = pl.ds(pl.multiple_of(i * BLOCK, BLOCK), BLOCK)
            keys = jnp.concatenate([ke[b] for b in near_blocks(j, i)], axis=0)
            s = lax.dot_general(
                q_ref[rows, columns], keys, (((1,), (1,)), ((), ())), preferred_element_type=jnp.float32
            )
            hidden = []
            for t in range(NS):
                hidden.append(jnp.where(c * PER_DEV + i - slash[j, t] >= 0, 0.0, NEG).astype(jnp.float32))
            for owner, there, distance in (
                (c_before, c > 0, PER_DEV + i - picked(j, c_before)),
                (c, c >= 0, i - picked(j, c)),
            ):
                shown = jnp.logical_and(jnp.logical_and(counts[j, owner] > 0, there), distance > 0)
                for t in range(NS):
                    shown = jnp.logical_and(shown, distance != slash[j, t])
                hidden.append(jnp.where(shown, 0.0, NEG).astype(jnp.float32))
            diagonal = [jnp.where(slash[j, t] == 0, 1.0, 0.0).astype(jnp.float32) for t in range(NS)] + [None] * 2
            for g in range(3):
                bias = jnp.where(low, hidden[2 * g], hidden[2 * g + 1])
                if g < 2:
                    bias = bias + causal * jnp.where(low, diagonal[2 * g], diagonal[2 * g + 1])
                part = slice(g * 2 * BLOCK, (g + 1) * 2 * BLOCK)
                near_scores[rows, part] = s[:, part] + bias
            return 0

        lax.fori_loop(0, PER_DEV, near, 0)

        def far(tile, _):
            rows = pl.ds(pl.multiple_of(tile * TILE, TILE), TILE)
            queries = q_ref[rows, columns]
            peak = functools.reduce(
                jnp.maximum, [near_scores[rows, g * 128 : (g + 1) * 128] for g in range(3)]
            )
            for part in range(4):
                at = part * 512
                s = lax.dot_general(
                    queries, kh[at : at + 512, :], (((1,), (1,)), ((), ())), preferred_element_type=jnp.float32
                )
                s = s + far_bias[j, 0:1, at : at + 512]
                scores[:, at : at + 512] = s
                for g in range(4):
                    peak = jnp.maximum(peak, s[:, g * 128 : (g + 1) * 128])
            peak = jnp.max(peak, axis=1, keepdims=True) * SCALE
            total = jnp.zeros((TILE, 2 * HEAD_SIZE), jnp.float32)
            for part in range(4):
                at = part * 512
                p = jnp.exp(scores[:, at : at + 512] * SCALE - peak).astype(jnp.bfloat16)
                total = total + jnp.dot(p, vh[at : at + 512, :], preferred_element_type=jnp.float32)
            numer[rows, :] = total
            near_probs[rows, :] = jnp.exp(near_scores[rows, :] * SCALE - peak).astype(jnp.bfloat16)
            return 0

        lax.fori_loop(0, TOKENS // TILE, far, 0)

        def finish(i, _):
            rows = pl.ds(pl.multiple_of(i * BLOCK, BLOCK), BLOCK)
            values = jnp.concatenate([ve[b] for b in near_blocks(j, i)], axis=0)
            both = jnp.concatenate([values, ones], axis=1)
            full = numer[rows, :] + jnp.dot(near_probs[rows, :], both, preferred_element_type=jnp.float32)
            att[hd, j, rows, :] = (full[:, :HEAD_SIZE] / full[:, HEAD_SIZE:]).astype(jnp.bfloat16)
            return 0

        lax.fori_loop(0, PER_DEV, finish, 0)

    def source(dy, other=False):
        return lax.rem(y + dy + NY, NY) * 2 + (1 - core if other else core)

    def part(j, which, src, first, size, device):
        ref = att.at[src, j, pl.ds(first, size)]
        return pltpu.make_async_remote_copy(
            src_ref=ref, dst_ref=ref, send_sem=ysend_sem.at[j, which], recv_sem=yrecv_sem.at[j, which],
            device_id=device, device_id_type=MESH,
        )

    HALF = TOKENS // 2
    plan = (
        (source(0), source(0, True), 0, TOKENS, sibling),
        (source(0), source(-1), 0, TOKENS, at_y(1)),
        (source(0), source(1), 0, TOKENS, at_y(-1)),
        (source(-1), source(-2), 0, HALF, at_y(1)),
        (source(1), source(2), HALF, HALF, at_y(-1)),
        (source(-1), source(-1, True), 0, TOKENS, sibling),
        (source(1), source(1, True), 0, TOKENS, sibling),
        (source(2), source(2, True), 0, HALF, sibling),
        (source(2), source(2, True), HALF, HALF, sibling),
    )

    def y_go(j, *which):
        for n in which:
            src, _, first, size, device = plan[n]
            part(j, n, src, first, size, device).start()

    def y_come(j, *which):
        for n in which:
            _, src, first, size, device = plan[n]
            part(j, n, src, first, size, device).wait_recv()

    def send(j):
        y_go(j, 1, 2, 0)

    def relay(j):
        y_come(j, 1)
        y_go(j, 3, 5)
        y_come(j, 2)
        y_go(j, 4, 6)

    def relay_far(j):
        y_come(j, 3)
        y_go(j, 7)
        y_come(j, 4)
        y_go(j, 8)

    def project(j):
        y_come(j, 0, 5, 6, 7, 8)

        def tile(t, _):
            rows = pl.ds(pl.multiple_of(t * TILE, TILE), TILE)
            a = jnp.concatenate([att[s, j, rows, :] for s in range(8)], axis=1)
            w = jnp.concatenate([w_ref[s, j] for s in range(8)], axis=0)
            acc[rows, :] += jnp.dot(a, w, preferred_element_type=jnp.float32)
            return 0

        lax.fori_loop(0, TOKENS // TILE, tile, 0)

    w_in.wait()

    def stage(j, _):
        @pl.when(j < HEADS)
        def _():
            attend(j)
            send(j)

        @pl.when(jnp.logical_and(j >= 1, j <= HEADS))
        def _():
            relay(j - 1)

        @pl.when(jnp.logical_and(j >= 2, j <= HEADS + 1))
        def _():
            relay_far(j - 2)
            project(j - 2)

        return 0

    lax.fori_loop(0, HEADS + 2, stage, 0)
    out_ref[...] = acc[...].astype(jnp.bfloat16)

    for kind, steps in ((a1, 2), (b1, 4), (a2, 4), (b2, 2)):
        for step in range(1, steps + 1):
            for way in (1, -1):
                kind(step, way, step - 1).wait_send()
    previous(ke, 24).wait_send()
    previous(ve, 25).wait_send()

    def drain(j, _):
        for n in range(9):
            src, _, first, size, device = plan[n]
            part(j, n, src, first, size, device).wait_send()
        return 0

    lax.fori_loop(0, HEADS, drain, 0)


def shards(queries, key_rows, value_rows, slash_offsets, union_blocks, head_picks, owner_counts, out_weight):
    bf16, f32 = jnp.bfloat16, jnp.float32
    smem = pl.BlockSpec(memory_space=pltpu.SMEM)
    hbm = pl.BlockSpec(memory_space=pl.ANY)
    vmem = pltpu.VMEM
    return pl.pallas_call(
        kernel,
        out_shape=jax.ShapeDtypeStruct((TOKENS, TOKENS), bf16),
        in_specs=[smem] * 4 + [hbm] * 4,
        out_specs=pl.BlockSpec(memory_space=pltpu.VMEM),
        scratch_shapes=[
            vmem((TOKENS, HEADS * HEAD_SIZE), bf16),
            vmem((PER_DEV, BLOCK, HEAD_SIZE), bf16),
            vmem((PER_DEV, BLOCK, HEAD_SIZE), bf16),
            vmem((2 * PER_DEV, BLOCK, HEAD_SIZE), bf16),
            vmem((2 * PER_DEV, BLOCK, HEAD_SIZE), bf16),
            vmem((8, HEADS, HEAD_SIZE, TOKENS), bf16),
            vmem((128, BLOCK, HEAD_SIZE), bf16),
            vmem((OWNERS * BLOCK, HEAD_SIZE), bf16),
            vmem((OWNERS * BLOCK, 2 * HEAD_SIZE), bf16),
            vmem((TILE, OWNERS * BLOCK), f32),
            vmem((TOKENS, NEAR), f32),
            vmem((TOKENS, NEAR), bf16),
            vmem((TOKENS, 2 * HEAD_SIZE), f32),
            vmem((8, HEADS, TOKENS, HEAD_SIZE), bf16),
            vmem((TOKENS, TOKENS), f32),
            vmem((HEADS, 8, OWNERS * BLOCK), f32),
            pltpu.SemaphoreType.DMA((6,)),
            pltpu.SemaphoreType.DMA((26,)),
            pltpu.SemaphoreType.DMA((26,)),
            pltpu.SemaphoreType.DMA((HEADS, 9)),
            pltpu.SemaphoreType.DMA((HEADS, 9)),
        ],
        compiler_params=pltpu.CompilerParams(
            collective_id=0, has_side_effects=True, vmem_limit_bytes=60 * 1024 * 1024
        ),
    )(
        slash_offsets, union_blocks.transpose(0, 2, 1), head_picks.transpose(0, 2, 1), owner_counts,
        queries, key_rows.reshape(PER_DEV, BLOCK, HEAD_SIZE), value_rows.reshape(PER_DEV, BLOCK, HEAD_SIZE),
        out_weight.reshape(8, HEADS, HEAD_SIZE, TOKENS),
    )


def solution(mesh):
    in_specs = (
        P("ctx", "head"), P("ctx", "head"), P("ctx", "head"), P("head", None),
        P("head", None, None), P("head", None, None), P("head", None), P(None, "head"),
    )
    return jax.shard_map(
        shards, mesh=mesh, in_specs=in_specs, out_specs=P("ctx", "head"), check_vma=False
    )
```

time: 190 us -> 80 us (0.42)
  Pallas kernels: 0 us -> 77.8 us
  waiting for transfers between devices: 68 us -> 0 us
  local copies, waits for them, and re-layouts: 56.4 us -> 1.87 us
  matrix products: 33 us -> 0 us
  between operations: 14.1 us -> 0.01 us
  other arithmetic: 13.2 us -> 0 us
  starting transfers between devices: 4.43 us -> 0 us
    pallas_call x0 -> x1, Pallas kernels: none -> 77.8 us  [shards(): pl.pallas_call(kernel, out_shape=jax.ShapeDtypeStruct((TOKENS, TOKENS), b...]
    all_gather x2 -> x0, waiting for transfers between devices: 68 us -> none  [the longest x1 35.2 us: shards(): lax.all_gather(attended, 'head', axis=1, tiled=True)]
    dot_general x17 -> x0, matrix products: 33 us -> none  [the longest x4 14.6 us: shards(): jnp.einsum('qd,kd->qk', query_head, vert_keys, preferred_element_type=jnp...]
    reshape x8 -> x0, local copies, waits for them, and re-layouts: 19.4 us -> none  [the longest x4 18.9 us: shards(): vert_mask = jnp.broadcast_to(block_mask[:, None, :, None], (per_dev, BLOC...]
    slice x6 -> x0, local copies, waits for them, and re-layouts: 11 us -> none  [the longest x4 5.9 us: shards(): vertical[:, :, 1].reshape(slot_count * BLOCK_TOKENS, HEAD_SIZE)]
    gather x16 -> x0, local copies, waits for them, and re-layouts: 9.76 us -> none  [the longest x8 5.42 us: shards(): slash_rows = group_slab[:, ext_index]]
    reduce_sum x8 -> x0, other arithmetic: 6.93 us -> none  [the longest x4 4.86 us: attend(): jnp.sum(weight_vert, axis=-1, keepdims=True)]
    unnamed x88 -> x1, local copies, waits for them, and re-layouts: 6.68 us -> 1.87 us
  transfers between devices with their start and end apart: 3 -> 0, of which waited for: 2 -> 0; matrix products, arithmetic and copies ran while one was open for 22% -> 0% of each run, Pallas kernels for 0% -> 0%
where the time goes in v1:
time: 80 us; the launch traced here: 79.7 us
  Pallas kernels  77.8 us (97%)
  local copies, waits for them, and re-layouts  1.87 us (2%)
    pallas_call x1, Pallas kernels, shards(): pl.pallas_call(kernel, out_shape=jax.ShapeDtypeStruct((TOKENS, TOKENS), b...  77.8 us
    unnamed x1, local copies, waits for them, and re-layouts  1.87 us

profile of v1, /device:TPU:1, one launch (start us, length us, event | category | flops | bytes accessed | tf_op | source)
XLA Modules:
  0.0 79.7 jit_solution(16714007242088594797)
XLA Ops:
  0.0 77.8 %shard_map.82 = bf16[512,512]{1,0:T(8,128)(2,1)} custom-call(s32[4,4]{1,0:T(4,128)} %slash.1, s32[1,2,32]{2,1,0:T(2,128)} %bitcast.11, s32[4,1,32]{2,1,0:T(1,128)} %bitcast.10, s32[4,32]{1,0:T(4,128)} %counts.1, bf16[512,512]{1,0:T(8,128)(2,1)} %q_hbm.1, bf16[8,64,128]{2,1,0:T(8,128)(2,1)} %bitcast.8, bf16[8,64,128]{2,1,0:T(8,128)(2,1)} %bitcast.9, ...), custom_call_target="tpu_custom_call" | custom-call | tf_op jit(solution)/shard_map/pallas_call | solution.py:360
  77.9 1.9 %copy.11 = bf16[512,512]{1,0:T(8,128)(2,1)} copy(bf16[512,512]{1,0:T(8,128)(2,1)} %shard_map.82) | data formatting | bytes 1048576

commit v2 on v1

v2 whole, which is shorter than its diff:
```python
import functools

import jax
import jax.numpy as jnp
from jax import lax
from jax.experimental import pallas as pl
from jax.experimental.pallas import tpu as pltpu
from jax.sharding import PartitionSpec as P

HEAD_SIZE = 128
BLOCK = 64
NS = 4
HEADS = 4
OWNERS = 32
PER_DEV = 8
TOKENS = 512
NX, NZ, NY = 4, 8, 4
TILE = 256
TILES = TOKENS // TILE
UNITS = HEADS * TILES
NEAR = 6 * BLOCK
NEG = -1e30
SCALE = HEAD_SIZE**-0.5
MESH = pl.DeviceIdType.MESH

PLACE = [0, 1, 3, 5, 7, 6, 4, 2]
GROUPS = ((0, 1), (1, 2), (3, 2), (5, 3))


def kernel(
    slash, union, picks, counts, q_hbm, k_hbm, v_hbm, w_hbm, out_ref,
    q_ref, k_own, v_own, ke, ve, w_ref, pieces, kh, vh, scores, near_peak, near_sum, att, acc,
    far_bias, local_sem, send_sem, recv_sem, ysend_sem, yrecv_sem,
):
    c = lax.axis_index("ctx")
    hd = lax.axis_index("head")
    x, z = c // NZ, lax.rem(c, NZ)
    y, core = hd // 2, lax.rem(hd, 2)

    def at_xz(dx, dz):
        return {"ctx": lax.rem(x + dx + NX, NX) * NZ + lax.rem(z + dz + NZ, NZ)}

    def at_y(dy):
        return {"head": lax.rem(y + dy + NY, NY) * 2 + core}

    sibling = {"head": y * 2 + 1 - core}
    after = {"ctx": lax.rem(c + 1, OWNERS)}
    before = {"ctx": lax.rem(c + OWNERS - 1, OWNERS)}

    k_pack = pltpu.make_async_copy(k_hbm, k_own, local_sem.at[0])
    v_pack = pltpu.make_async_copy(v_hbm, v_own, local_sem.at[1])
    k_in = pltpu.make_async_copy(k_hbm, ke.at[pl.ds(PER_DEV, PER_DEV)], local_sem.at[2])
    v_in = pltpu.make_async_copy(v_hbm, ve.at[pl.ds(PER_DEV, PER_DEV)], local_sem.at[3])
    q_in = pltpu.make_async_copy(q_hbm, q_ref, local_sem.at[4])
    w_in = pltpu.make_async_copy(w_hbm, w_ref, local_sem.at[5])
    for copy in (k_pack, v_pack, k_in, v_in, q_in, w_in):
        copy.start()

    barrier = pltpu.get_barrier_semaphore()
    peers = [at_xz(0, dz) for dz in range(1, NZ)]
    peers += [at_xz(1, 0), at_xz(-1, 0), after, before, sibling, at_y(1), at_y(-1)]
    for peer in peers:
        pl.semaphore_signal(barrier, inc=1, device_id=peer, device_id_type=MESH)

    vh[:, HEAD_SIZE:] = jnp.ones((OWNERS * BLOCK, HEAD_SIZE), jnp.bfloat16)
    acc[...] = jnp.zeros_like(acc)

    def owner_of(dx, dz):
        return lax.rem(x + dx, NX) * NZ + lax.rem(z + dz, NZ)

    for dx in range(NX):
        for dz in range(NZ):
            o, at = owner_of(dx, dz), (dx * NZ + PLACE[dz]) * BLOCK
            for j in range(HEADS):
                seen = jnp.logical_and(counts[j, o] > 0, o <= c - 2)
                value = jnp.where(seen, 0.0, NEG).astype(jnp.float32)
                far_bias[j, :, at : at + BLOCK] = jnp.full((8, BLOCK), value, jnp.float32)

    k_pack.wait()
    v_pack.wait()
    for u in range(2):
        pieces[0, 2 * u] = k_own[union[0, u, c]]
        pieces[0, 2 * u + 1] = v_own[union[0, u, c]]

    def remote(src, dst, sem, device):
        return pltpu.make_async_remote_copy(
            src_ref=src, dst_ref=dst, send_sem=send_sem.at[sem], recv_sem=recv_sem.at[sem],
            device_id=device, device_id_type=MESH,
        )

    def along_z(dz):
        return remote(pieces.at[0], pieces.at[PLACE[NZ - dz]], dz - 1, at_xz(0, dz))

    def along_x(group, way):
        first, size = GROUPS[group]
        side = NX - 1 if way > 0 else 1
        return remote(
            pieces.at[pl.ds(first, size)], pieces.at[pl.ds(side * NZ + first, size)],
            7 + 2 * group + (way > 0), at_xz(way, 0),
        )

    def on_x(group, way):
        first, size = GROUPS[group]
        side, half = (NX - 1, 0) if way > 0 else (1, 2)
        return remote(
            pieces.at[pl.ds(side * NZ + first, size), pl.ds(half, 2)],
            pieces.at[pl.ds(2 * NZ + first, size), pl.ds(half, 2)],
            15 + 2 * group + (way > 0), at_xz(way, 0),
        )

    def previous(ref, sem):
        return remote(ref.at[pl.ds(PER_DEV, PER_DEV)], ref.at[pl.ds(0, PER_DEV)], sem, after)

    def z_come(*steps):
        for dz in steps:
            along_z(dz).wait_recv()

    def both_ways(kind, group):
        kind(group, 1).start()
        kind(group, -1).start()

    def x_come(kind, group):
        kind(group, 1).wait_recv()
        kind(group, -1).wait_recv()

    lane = lax.broadcasted_iota(jnp.int32, (BLOCK, 2 * BLOCK), 1)
    row = lax.broadcasted_iota(jnp.int32, (BLOCK, 2 * BLOCK), 0)
    low = lane < BLOCK
    causal = jnp.where((lane % BLOCK) <= row, 0.0, NEG).astype(jnp.float32)
    c_before = jnp.maximum(c - 1, 0)
    ones = jnp.ones((NEAR, HEAD_SIZE), jnp.bfloat16)

    def picked(j, owner):
        first, second = union[0, 0, owner], union[0, 1, owner]
        return first + picks[j, 0, owner] * (second - first)

    def near(i, _):
        rows = pl.ds(pl.multiple_of(i * BLOCK, BLOCK), BLOCK)
        for j in range(HEADS):
            blocks = [i + PER_DEV - slash[j, s] for s in range(NS)]
            blocks += [picked(j, c_before), PER_DEV + picked(j, c)]
            hidden = []
            for t in range(NS):
                hidden.append(jnp.where(c * PER_DEV + i - slash[j, t] >= 0, 0.0, NEG).astype(jnp.float32))
            for owner, there, distance in (
                (c_before, c > 0, PER_DEV + i - blocks[4]),
                (c, c >= 0, PER_DEV + i - blocks[5]),
            ):
                shown = jnp.logical_and(jnp.logical_and(counts[j, owner] > 0, there), distance > 0)
                for t in range(NS):
                    shown = jnp.logical_and(shown, distance != slash[j, t])
                hidden.append(jnp.where(shown, 0.0, NEG).astype(jnp.float32))
            diagonal = [jnp.where(slash[j, t] == 0, 1.0, 0.0).astype(jnp.float32) for t in range(NS)]
            keys = jnp.concatenate([ke[b] for b in blocks], axis=0)
            s = lax.dot_general(
                q_ref[rows, j * HEAD_SIZE : (j + 1) * HEAD_SIZE], keys, (((1,), (1,)), ((), ())),
                preferred_element_type=jnp.float32,
            )
            parts = []
            for g in range(3):
                bias = jnp.where(low, hidden[2 * g], hidden[2 * g + 1])
                if g < 2:
                    bias = bias + causal * jnp.where(low, diagonal[2 * g], diagonal[2 * g + 1])
                parts.append(s[:, g * 2 * BLOCK : (g + 1) * 2 * BLOCK] + bias)
            peak = jnp.max(functools.reduce(jnp.maximum, parts), axis=1, keepdims=True)
            near_peak[j, rows, :] = jnp.broadcast_to(peak, (BLOCK, HEAD_SIZE))
            peak = peak * SCALE
            p = jnp.concatenate([jnp.exp(part * SCALE - peak).astype(jnp.bfloat16) for part in parts], axis=1)
            values = jnp.concatenate([jnp.concatenate([ve[b] for b in blocks], axis=0), ones], axis=1)
            near_sum[j, rows, :] = jnp.dot(p, values, preferred_element_type=jnp.float32)
        return 0

    def near_rows(first, last):
        lax.fori_loop(first, last, near, 0)

    pl.semaphore_wait(barrier, len(peers))

    both_ways(along_x, 0)
    for dz in (1, 7, 2, 6):
        along_z(dz).start()
    k_in.wait()
    previous(ke, 23).start()
    for dz in (3, 5, 4):
        along_z(dz).start()
    v_in.wait()
    previous(ve, 24).start()
    q_in.wait()

    z_come(1, 7)
    both_ways(along_x, 1)
    x_come(along_x, 0)
    both_ways(on_x, 0)
    z_come(2, 6)
    both_ways(along_x, 2)
    z_come(3, 5, 4)
    both_ways(along_x, 3)
    x_come(along_x, 1)
    both_ways(on_x, 1)
    previous(ke, 23).wait_recv()
    previous(ve, 24).wait_recv()
    near_rows(0, 2)
    x_come(along_x, 2)
    both_ways(on_x, 2)
    near_rows(2, 4)
    x_come(along_x, 3)
    both_ways(on_x, 3)
    near_rows(4, 8)
    for group in range(4):
        x_come(on_x, group)
    w_in.wait()

    def attend(unit):
        j, tile = unit // TILES, lax.rem(unit, TILES)
        columns = pl.ds(pl.multiple_of(j * HEAD_SIZE, HEAD_SIZE), HEAD_SIZE)

        @pl.when(tile == 0)
        def _():
            for dx in range(NX):
                for dz in range(NZ):
                    slot = dx * NZ + PLACE[dz]
                    pick = picks[j, 0, owner_of(dx, dz)]
                    kh[slot * BLOCK : (slot + 1) * BLOCK, :] = pieces[slot, 2 * pick]
                    vh[slot * BLOCK : (slot + 1) * BLOCK, :HEAD_SIZE] = pieces[slot, 2 * pick + 1]

        rows = pl.ds(pl.multiple_of(tile * TILE, TILE), TILE)
        queries = q_ref[rows, columns]
        nearest = near_peak[j, rows, :]
        peak = nearest
        for part in range(4):
            at = part * 512
            s = lax.dot_general(
                queries, kh[at : at + 512, :], (((1,), (1,)), ((), ())), preferred_element_type=jnp.float32
            )
            s = s + far_bias[j, 0:1, at : at + 512]
            scores[:, at : at + 512] = s
            for g in range(4):
                peak = jnp.maximum(peak, s[:, g * 128 : (g + 1) * 128])
        peak = jnp.max(peak, axis=1, keepdims=True) * SCALE
        shrink = jnp.exp(nearest * SCALE - peak)
        total = near_sum[j, rows, :] * jnp.concatenate([shrink, shrink], axis=1)
        for part in range(4):
            at = part * 512
            p = jnp.exp(scores[:, at : at + 512] * SCALE - peak).astype(jnp.bfloat16)
            total = total + jnp.dot(p, vh[at : at + 512, :], preferred_element_type=jnp.float32)
        att[hd, j, rows, :] = (total[:, :HEAD_SIZE] / total[:, HEAD_SIZE:]).astype(jnp.bfloat16)

    def source(dy, other=False):
        return lax.rem(y + dy + NY, NY) * 2 + (1 - core if other else core)

    HALF = TILE // 2
    plan = (
        (source(0), source(0, True), 0, TILE, sibling),
        (source(0), source(-1), 0, TILE, at_y(1)),
        (source(0), source(1), 0, TILE, at_y(-1)),
        (source(-1), source(-2), 0, HALF, at_y(1)),
        (source(1), source(2), HALF, HALF, at_y(-1)),
        (source(-1), source(-1, True), 0, TILE, sibling),
        (source(1), source(1, True), 0, TILE, sibling),
        (source(2), source(2, True), 0, HALF, sibling),
        (source(2), source(2, True), HALF, HALF, sibling),
    )

    def exchange(unit, which, incoming):
        out, come, first, size, device = plan[which]
        j, tile = unit // TILES, lax.rem(unit, TILES)
        ref = att.at[come if incoming else out, j, pl.ds(pl.multiple_of(tile * TILE, TILE) + first, size)]
        return pltpu.make_async_remote_copy(
            src_ref=ref, dst_ref=ref, send_sem=ysend_sem.at[unit, which], recv_sem=yrecv_sem.at[unit, which],
            device_id=device, device_id_type=MESH,
        )

    def y_go(unit, *which):
        for n in which:
            exchange(unit, n, False).start()

    def y_come(unit, *which):
        for n in which:
            exchange(unit, n, True).wait_recv()

    def relay(unit):
        y_come(unit, 1)
        y_go(unit, 3, 5)
        y_come(unit, 2)
        y_go(unit, 4, 6)

    def relay_far(unit):
        y_come(unit, 3)
        y_go(unit, 7)
        y_come(unit, 4)
        y_go(unit, 8)

    def project(unit):
        y_come(unit, 0, 5, 6, 7, 8)
        j, tile = unit // TILES, lax.rem(unit, TILES)
        rows = pl.ds(pl.multiple_of(tile * TILE, TILE), TILE)
        a = jnp.concatenate([att[s, j, rows, :] for s in range(8)], axis=1)
        w = jnp.concatenate([w_ref[s, j] for s in range(8)], axis=0)
        acc[rows, :] += jnp.dot(a, w, preferred_element_type=jnp.float32)

    def stage(step, _):
        @pl.when(step < UNITS)
        def _():
            attend(step)
            y_go(step, 1, 2, 0)

        @pl.when(jnp.logical_and(step >= 2, step < UNITS + 2))
        def _():
            relay(step - 2)

        @pl.when(jnp.logical_and(step >= 4, step < UNITS + 4))
        def _():
            relay_far(step - 4)

        @pl.when(step >= 5)
        def _():
            project(step - 5)

        return 0

    lax.fori_loop(0, UNITS + 5, stage, 0)
    out_ref[...] = acc[...].astype(jnp.bfloat16)

    for dz in range(1, NZ):
        along_z(dz).wait_send()
    for group in range(4):
        for way in (1, -1):
            along_x(group, way).wait_send()
            on_x(group, way).wait_send()
    previous(ke, 23).wait_send()
    previous(ve, 24).wait_send()

    def drain(unit, _):
        for n in range(9):
            exchange(unit, n, False).wait_send()
        return 0

    lax.fori_loop(0, UNITS, drain, 0)


def shards(queries, key_rows, value_rows, slash_offsets, union_blocks, head_picks, owner_counts, out_weight):
    bf16, f32 = jnp.bfloat16, jnp.float32
    smem = pl.BlockSpec(memory_space=pltpu.SMEM)
    hbm = pl.BlockSpec(memory_space=pl.ANY)
    vmem, dma = pltpu.VMEM, pltpu.SemaphoreType.DMA
    blocks = (PER_DEV, BLOCK, HEAD_SIZE)
    return pl.pallas_call(
        kernel,
        out_shape=jax.ShapeDtypeStruct((TOKENS, TOKENS), bf16),
        in_specs=[smem] * 4 + [hbm] * 4,
        out_specs=pl.BlockSpec(memory_space=pltpu.VMEM),
        scratch_shapes=[
            vmem((TOKENS, HEADS * HEAD_SIZE), bf16),
            vmem(blocks, bf16),
            vmem(blocks, bf16),
            vmem((2 * PER_DEV, BLOCK, HEAD_SIZE), bf16),
            vmem((2 * PER_DEV, BLOCK, HEAD_SIZE), bf16),
            vmem((8, HEADS, HEAD_SIZE, TOKENS), bf16),
            vmem((OWNERS, 4, BLOCK, HEAD_SIZE), bf16),
            vmem((OWNERS * BLOCK, HEAD_SIZE), bf16),
            vmem((OWNERS * BLOCK, 2 * HEAD_SIZE), bf16),
            vmem((TILE, OWNERS * BLOCK), f32),
            vmem((HEADS, TOKENS, HEAD_SIZE), f32),
            vmem((HEADS, TOKENS, 2 * HEAD_SIZE), f32),
            vmem((8, HEADS, TOKENS, HEAD_SIZE), bf16),
            vmem((TOKENS, TOKENS), f32),
            vmem((HEADS, 8, OWNERS * BLOCK), f32),
            dma((6,)),
            dma((25,)),
            dma((25,)),
            dma((UNITS, 9)),
            dma((UNITS, 9)),
        ],
        compiler_params=pltpu.CompilerParams(
            collective_id=0, has_side_effects=True, vmem_limit_bytes=60 * 1024 * 1024
        ),
    )(
        slash_offsets, union_blocks.transpose(0, 2, 1), head_picks.transpose(0, 2, 1), owner_counts,
        queries, key_rows.reshape(blocks), value_rows.reshape(blocks),
        out_weight.reshape(8, HEADS, HEAD_SIZE, TOKENS),
    )


def solution(mesh):
    in_specs = (
        P("ctx", "head"), P("ctx", "head"), P("ctx", "head"), P("head", None),
        P("head", None, None), P("head", None, None), P("head", None), P(None, "head"),
    )
    return jax.shard_map(
        shards, mesh=mesh, in_specs=in_specs, out_specs=P("ctx", "head"), check_vma=False
    )
```

time: 80 us -> 70.2 us (0.88)
  Pallas kernels: 77.8 us -> 68.2 us
    pallas_call x1, Pallas kernels: 77.8 us -> 68.2 us  [shards(): pl.pallas_call(kernel, out_shape=jax.ShapeDtypeStruct((TOKENS, TOKENS), b...]
where the time goes in v2:
time: 70.2 us; the launch traced here: 70.1 us
  Pallas kernels  68.2 us (97%)
  local copies, waits for them, and re-layouts  1.87 us (3%)
    pallas_call x1, Pallas kernels, shards(): pl.pallas_call(kernel, out_shape=jax.ShapeDtypeStruct((TOKENS, TOKENS), b...  68.2 us
    unnamed x1, local copies, waits for them, and re-layouts  1.87 us

profile of v2, /device:TPU:1, one launch (start us, length us, event | category | flops | bytes accessed | tf_op | source)
XLA Modules:
  0.0 70.1 jit_solution(10415416972490961399)
XLA Ops:
  0.0 68.2 %shard_map.82 = bf16[512,512]{1,0:T(8,128)(2,1)} custom-call(s32[4,4]{1,0:T(4,128)} %slash.1, s32[1,2,32]{2,1,0:T(2,128)} %bitcast.11, s32[4,1,32]{2,1,0:T(1,128)} %bitcast.10, s32[4,32]{1,0:T(4,128)} %counts.1, bf16[512,512]{1,0:T(8,128)(2,1)} %q_hbm.1, bf16[8,64,128]{2,1,0:T(8,128)(2,1)} %bitcast.8, bf16[8,64,128]{2,1,0:T(8,128)(2,1)} %bitcast.9, ...), custom_call_target="tpu_custom_call" | custom-call | tf_op jit(solution)/shard_map/pallas_call | solution.py:346
  68.2 1.9 %copy.11 = bf16[512,512]{1,0:T(8,128)(2,1)} copy(bf16[512,512]{1,0:T(8,128)(2,1)} %shard_map.82) | data formatting | bytes 1048576

commit v3 on v2

--- a/solution.py
+++ b/solution.py
@@ -18,6 +18,7 @@
 TILE = 256
 TILES = TOKENS // TILE
 UNITS = HEADS * TILES
+PART = 512
 NEAR = 6 * BLOCK
 NEG = -1e30
 SCALE = HEAD_SIZE**-0.5
@@ -29,7 +30,7 @@
 
 def kernel(
     slash, union, picks, counts, q_hbm, k_hbm, v_hbm, w_hbm, out_ref,
-    q_ref, k_own, v_own, ke, ve, w_ref, pieces, kh, vh, scores, near_peak, near_sum, att, acc,
+    q_ref, k_own, v_own, ke, ve, w_ref, pieces, kt, vh, scores, near_peak, near_total, near_sum, att, acc,
     far_bias, local_sem, send_sem, recv_sem, ysend_sem, yrecv_sem,
 ):
     c = lax.axis_index("ctx")
@@ -57,12 +58,11 @@
         copy.start()
 
     barrier = pltpu.get_barrier_semaphore()
-    peers = [at_xz(0, dz) for dz in range(1, NZ)]
+    peers = [at_xz(0, dz) for dz in (1, 2, 6, 7)]
     peers += [at_xz(1, 0), at_xz(-1, 0), after, before, sibling, at_y(1), at_y(-1)]
     for peer in peers:
         pl.semaphore_signal(barrier, inc=1, device_id=peer, device_id_type=MESH)
 
-    vh[:, HEAD_SIZE:] = jnp.ones((OWNERS * BLOCK, HEAD_SIZE), jnp.bfloat16)
     acc[...] = jnp.zeros_like(acc)
 
     def owner_of(dx, dz):
@@ -78,9 +78,10 @@
 
     k_pack.wait()
     v_pack.wait()
-    for u in range(2):
-        pieces[0, 2 * u] = k_own[union[0, u, c]]
-        pieces[0, 2 * u + 1] = v_own[union[0, u, c]]
+    first, second, pick = union[0, 0, c], union[0, 1, c], picks[0, 0, c]
+    for half, block in enumerate((first + pick * (second - first), second + pick * (first - second))):
+        pieces[half, 0, 0] = k_own[block]
+        pieces[half, 0, 1] = v_own[block]
 
     def remote(src, dst, sem, device):
         return pltpu.make_async_remote_copy(
@@ -88,47 +89,84 @@
             device_id=device, device_id_type=MESH,
         )
 
-    def along_z(dz):
-        return remote(pieces.at[0], pieces.at[PLACE[NZ - dz]], dz - 1, at_xz(0, dz))
-
-    def along_x(group, way):
+    def along_z(half, dz):
+        return remote(pieces.at[half, 0], pieces.at[half, PLACE[NZ - dz]], 24 * half + dz - 1, at_xz(0, dz))
+
+    def z_on(half, way):
+        src, dst = (PLACE[6], PLACE[5]) if way > 0 else (PLACE[2], PLACE[3])
+        return remote(
+            pieces.at[half, src], pieces.at[half, dst], 24 * half + (2 if way > 0 else 4), at_xz(0, way)
+        )
+
+    def z_across(half, way):
+        src, kind = (PLACE[6], 0) if way > 0 else (PLACE[2], 1)
+        return remote(
+            pieces.at[half, src, kind], pieces.at[half, PLACE[4], kind],
+            24 * half + (3 if way > 0 else 7), at_xz(0, 2 * way),
+        )
+
+    def along_x(half, group, way):
         first, size = GROUPS[group]
         side = NX - 1 if way > 0 else 1
         return remote(
-            pieces.at[pl.ds(first, size)], pieces.at[pl.ds(side * NZ + first, size)],
-            7 + 2 * group + (way > 0), at_xz(way, 0),
-        )
-
-    def on_x(group, way):
+            pieces.at[half, pl.ds(first, size)], pieces.at[half, pl.ds(side * NZ + first, size)],
+            24 * half + 8 + 2 * group + (way > 0), at_xz(way, 0),
+        )
+
+    def on_x(half, group, way):
         first, size = GROUPS[group]
-        side, half = (NX - 1, 0) if way > 0 else (1, 2)
+        side, kind = (NX - 1, 0) if way > 0 else (1, 1)
         return remote(
-            pieces.at[pl.ds(side * NZ + first, size), pl.ds(half, 2)],
-            pieces.at[pl.ds(2 * NZ + first, size), pl.ds(half, 2)],
-            15 + 2 * group + (way > 0), at_xz(way, 0),
+            pieces.at[half, pl.ds(side * NZ + first, size), kind],
+            pieces.at[half, pl.ds(2 * NZ + first, size), kind],
+            24 * half + 16 + 2 * group + (way > 0), at_xz(way, 0),
         )
 
     def previous(ref, sem):
         return remote(ref.at[pl.ds(PER_DEV, PER_DEV)], ref.at[pl.ds(0, PER_DEV)], sem, after)
 
-    def z_come(*steps):
+    def z_go(half, *steps):
         for dz in steps:
-            along_z(dz).wait_recv()
-
-    def both_ways(kind, group):
-        kind(group, 1).start()
-        kind(group, -1).start()
-
-    def x_come(kind, group):
-        kind(group, 1).wait_recv()
-        kind(group, -1).wait_recv()
+            along_z(half, dz).start()
+
+    def z_come(half, *steps):
+        for dz in steps:
+            along_z(half, dz).wait_recv()
+
+    def x_go(kind, half, group):
+        kind(half, group, 1).start()
+        kind(half, group, -1).start()
+
+    def x_come(kind, half, group):
+        kind(half, group, 1).wait_recv()
+        kind(half, group, -1).wait_recv()
+
+    def z_then_x(half, group, *steps):
+        z_come(half, *steps)
+        x_go(along_x, half, group)
+
+    def z_far_go(half):
+        z_come(half, 2, 6)
+        for way in (1, -1):
+            z_on(half, way).start()
+            z_across(half, way).start()
+        x_go(along_x, half, 2)
+
+    def z_far_come(half):
+        for way in (1, -1):
+            z_on(half, way).wait_recv()
+            z_across(half, way).wait_recv()
+        x_go(along_x, half, 3)
+
+    def further(half, group):
+        x_come(along_x, half, group)
+        x_go(on_x, half, group)
 
     lane = lax.broadcasted_iota(jnp.int32, (BLOCK, 2 * BLOCK), 1)
     row = lax.broadcasted_iota(jnp.int32, (BLOCK, 2 * BLOCK), 0)
     low = lane < BLOCK
     causal = jnp.where((lane % BLOCK) <= row, 0.0, NEG).astype(jnp.float32)
     c_before = jnp.maximum(c - 1, 0)
-    ones = jnp.ones((NEAR, HEAD_SIZE), jnp.bfloat16)
 
     def picked(j, owner):
         first, second = union[0, 0, owner], union[0, 1, owner]
@@ -165,8 +203,10 @@
             peak = jnp.max(functools.reduce(jnp.maximum, parts), axis=1, keepdims=True)
             near_peak[j, rows, :] = jnp.broadcast_to(peak, (BLOCK, HEAD_SIZE))
             peak = peak * SCALE
-            p = jnp.concatenate([jnp.exp(part * SCALE - peak).astype(jnp.bfloat16) for part in parts], axis=1)
-            values = jnp.concatenate([jnp.concatenate([ve[b] for b in blocks], axis=0), ones], axis=1)
+            weights = [jnp.exp(part * SCALE - peak) for part in parts]
+            near_total[j, rows, :] = functools.reduce(jnp.add, weights)
+            p = jnp.concatenate([w.astype(jnp.bfloat16) for w in weights], axis=1)
+            values = jnp.concatenate([ve[b] for b in blocks], axis=0)
             near_sum[j, rows, :] = jnp.dot(p, values, preferred_element_type=jnp.float32)
         return 0
 
@@ -175,74 +215,96 @@
 
     pl.semaphore_wait(barrier, len(peers))
 
-    both_ways(along_x, 0)
-    for dz in (1, 7, 2, 6):
-        along_z(dz).start()
+    x_go(along_x, 0, 0)
+    z_go(0, 2, 6, 1, 7)
     k_in.wait()
-    previous(ke, 23).start()
-    for dz in (3, 5, 4):
-        along_z(dz).start()
+    previous(ke, 48).start()
     v_in.wait()
-    previous(ve, 24).start()
+    previous(ve, 49).start()
+    z_far_go(0)
+    z_then_x(0, 1, 1, 7)
+    further(0, 0)
+    z_far_come(0)
+    x_go(along_x, 1, 0)
+    z_go(1, 2, 6, 1, 7)
+    further(0, 1)
+    further(0, 2)
     q_in.wait()
-
-    z_come(1, 7)
-    both_ways(along_x, 1)
-    x_come(along_x, 0)
-    both_ways(on_x, 0)
-    z_come(2, 6)
-    both_ways(along_x, 2)
-    z_come(3, 5, 4)
-    both_ways(along_x, 3)
-    x_come(along_x, 1)
-    both_ways(on_x, 1)
-    previous(ke, 23).wait_recv()
-    previous(ve, 24).wait_recv()
-    near_rows(0, 2)
-    x_come(along_x, 2)
-    both_ways(on_x, 2)
-    near_rows(2, 4)
-    x_come(along_x, 3)
-    both_ways(on_x, 3)
-    near_rows(4, 8)
+    previous(ke, 48).wait_recv()
+    previous(ve, 49).wait_recv()
+    near_rows(0, 1)
+    further(0, 3)
+    near_rows(1, 2)
+    z_far_go(1)
+    near_rows(2, 3)
+    z_then_x(1, 1, 1, 7)
+    further(1, 0)
+    near_rows(3, 4)
+    z_far_come(1)
+    near_rows(4, 5)
+    further(1, 1)
+    near_rows(5, 6)
+    further(1, 2)
+    near_rows(6, 7)
+    further(1, 3)
+    near_rows(7, 8)
     for group in range(4):
-        x_come(on_x, group)
-    w_in.wait()
-
-    def attend(unit):
-        j, tile = unit // TILES, lax.rem(unit, TILES)
+        x_come(on_x, 0, group)
+
+    def rest():
+        for group in range(4):
+            x_come(on_x, 1, group)
+        w_in.wait()
+
+    def gather_blocks(which):
+        for dx in range(NX):
+            for place in range(0, NZ, 2):
+                slot = dx * NZ + place
+                halves = [which(owner_of(dx, PLACE.index(place + n))) for n in range(2)]
+                keys = [pieces[halves[n], slot + n, 0] for n in range(2)]
+                columns = slice(slot * BLOCK, (slot + 2) * BLOCK)
+                kt[:, columns] = jnp.concatenate(keys, axis=0).T
+                for n in range(2):
+                    vh[(slot + n) * BLOCK : (slot + n + 1) * BLOCK, :] = pieces[halves[n], slot + n, 1]
+
+    def attend(j):
+        @pl.when(j == 0)
+        def _():
+            gather_blocks(lambda owner: 0)
+
+        @pl.when(j > 0)
+        def _():
+            def which(owner):
+                apart = picks[j, 0, owner] - picks[0, 0, owner]
+                return apart * apart
+
+            gather_blocks(which)
+
         columns = pl.ds(pl.multiple_of(j * HEAD_SIZE, HEAD_SIZE), HEAD_SIZE)
 
-        @pl.when(tile == 0)
-        def _():
-            for dx in range(NX):
-                for dz in range(NZ):
-                    slot = dx * NZ + PLACE[dz]
-                    pick = picks[j, 0, owner_of(dx, dz)]
-                    kh[slot * BLOCK : (slot + 1) * BLOCK, :] = pieces[slot, 2 * pick]
-                    vh[slot * BLOCK : (slot + 1) * BLOCK, :HEAD_SIZE] = pieces[slot, 2 * pick + 1]
-
-        rows = pl.ds(pl.multiple_of(tile * TILE, TILE), TILE)
-        queries = q_ref[rows, columns]
-        nearest = near_peak[j, rows, :]
-        peak = nearest
-        for part in range(4):
-            at = part * 512
-            s = lax.dot_general(
-                queries, kh[at : at + 512, :], (((1,), (1,)), ((), ())), preferred_element_type=jnp.float32
-            )
-            s = s + far_bias[j, 0:1, at : at + 512]
-            scores[:, at : at + 512] = s
-            for g in range(4):
-                peak = jnp.maximum(peak, s[:, g * 128 : (g + 1) * 128])
-        peak = jnp.max(peak, axis=1, keepdims=True) * SCALE
-        shrink = jnp.exp(nearest * SCALE - peak)
-        total = near_sum[j, rows, :] * jnp.concatenate([shrink, shrink], axis=1)
-        for part in range(4):
-            at = part * 512
-            p = jnp.exp(scores[:, at : at + 512] * SCALE - peak).astype(jnp.bfloat16)
-            total = total + jnp.dot(p, vh[at : at + 512, :], preferred_element_type=jnp.float32)
-        att[hd, j, rows, :] = (total[:, :HEAD_SIZE] / total[:, HEAD_SIZE:]).astype(jnp.bfloat16)
+        for tile in range(TILES):
+            rows = slice(tile * TILE, (tile + 1) * TILE)
+            queries = q_ref[rows, columns]
+            nearest = near_peak[j, rows, :]
+            peak = nearest
+            for at in range(0, OWNERS * BLOCK, PART):
+                s = jnp.dot(queries, kt[:, at : at + PART], preferred_element_type=jnp.float32)
+                s = s + far_bias[j, 0:1, at : at + PART]
+                scores[rows, at : at + PART] = s
+                for g in range(0, PART, 128):
+                    peak = jnp.maximum(peak, s[:, g : g + 128])
+            peak = jnp.max(peak, axis=1, keepdims=True) * SCALE
+            shrink = jnp.exp(nearest * SCALE - peak)
+            total = near_total[j, rows, :] * shrink
+            numer = near_sum[j, rows, :] * shrink
+            for at in range(0, OWNERS * BLOCK, PART):
+                weights = jnp.exp(scores[rows, at : at + PART] * SCALE - peak)
+                for g in range(0, PART, 128):
+                    total = total + weights[:, g : g + 128]
+                numer = numer + jnp.dot(
+                    weights.astype(jnp.bfloat16), vh[at : at + PART, :], preferred_element_type=jnp.float32
+                )
+            att[hd, j, rows, :] = (numer / jnp.sum(total, axis=1, keepdims=True)).astype(jnp.bfloat16)
 
     def source(dy, other=False):
         return lax.rem(y + dy + NY, NY) * 2 + (1 - core if other else core)
@@ -297,37 +359,49 @@
         w = jnp.concatenate([w_ref[s, j] for s in range(8)], axis=0)
         acc[rows, :] += jnp.dot(a, w, preferred_element_type=jnp.float32)
 
+    def of_head(do, head):
+        for tile in range(TILES):
+            do(TILES * head + tile)
+
     def stage(step, _):
-        @pl.when(step < UNITS)
+        @pl.when(step == 1)
+        def _():
+            rest()
+
+        @pl.when(step < HEADS)
         def _():
             attend(step)
-            y_go(step, 1, 2, 0)
-
-        @pl.when(jnp.logical_and(step >= 2, step < UNITS + 2))
-        def _():
-            relay(step - 2)
-
-        @pl.when(jnp.logical_and(step >= 4, step < UNITS + 4))
-        def _():
-            relay_far(step - 4)
-
-        @pl.when(step >= 5)
-        def _():
-            project(step - 5)
+            of_head(lambda unit: y_go(unit, 1, 2, 0), step)
+
+        @pl.when(jnp.logical_or(step == 1, jnp.logical_and(step >= 3, step < HEADS + 2)))
+        def _():
+            of_head(relay, jnp.where(step == 1, 0, step - 2))
+
+        @pl.when(jnp.logical_or(step == 2, jnp.logical_and(step >= 5, step < HEADS + 4)))
+        def _():
+            of_head(relay_far, jnp.where(step == 2, 0, step - 4))
+
+        @pl.when(jnp.logical_or(step == 3, step >= 6))
+        def _():
+            of_head(project, jnp.where(step == 3, 0, step - 5))
 
         return 0
 
-    lax.fori_loop(0, UNITS + 5, stage, 0)
+    lax.fori_loop(0, HEADS + 5, stage, 0)
     out_ref[...] = acc[...].astype(jnp.bfloat16)
 
-    for dz in range(1, NZ):
-        along_z(dz).wait_send()
-    for group in range(4):
+    for half in range(2):
+        for dz in (1, 2, 6, 7):
+            along_z(half, dz).wait_send()
         for way in (1, -1):
-            along_x(group, way).wait_send()
-            on_x(group, way).wait_send()
-    previous(ke, 23).wait_send()
-    previous(ve, 24).wait_send()
+            z_on(half, way).wait_send()
+            z_across(half, way).wait_send()
+        for group in range(4):
+            for way in (1, -1):
+                along_x(half, group, way).wait_send()
+                on_x(half, group, way).wait_send()
+    previous(ke, 48).wait_send()
+    previous(ve, 49).wait_send()
 
     def drain(unit, _):
         for n in range(9):
@@ -355,18 +429,19 @@
             vmem((2 * PER_DEV, BLOCK, HEAD_SIZE), bf16),
             vmem((2 * PER_DEV, BLOCK, HEAD_SIZE), bf16),
             vmem((8, HEADS, HEAD_SIZE, TOKENS), bf16),
-            vmem((OWNERS, 4, BLOCK, HEAD_SIZE), bf16),
+            vmem((2, OWNERS, 2, BLOCK, HEAD_SIZE), bf16),
+            vmem((HEAD_SIZE, OWNERS * BLOCK), bf16),
             vmem((OWNERS * BLOCK, HEAD_SIZE), bf16),
-            vmem((OWNERS * BLOCK, 2 * HEAD_SIZE), bf16),
-            vmem((TILE, OWNERS * BLOCK), f32),
+            vmem((TOKENS, OWNERS * BLOCK), f32),
             vmem((HEADS, TOKENS, HEAD_SIZE), f32),
-            vmem((HEADS, TOKENS, 2 * HEAD_SIZE), f32),
+            vmem((HEADS, TOKENS, HEAD_SIZE), f32),
+            vmem((HEADS, TOKENS, HEAD_SIZE), f32),
             vmem((8, HEADS, TOKENS, HEAD_SIZE), bf16),
             vmem((TOKENS, TOKENS), f32),
             vmem((HEADS, 8, OWNERS * BLOCK), f32),
             dma((6,)),
-            dma((25,)),
-            dma((25,)),
+            dma((50,)),
+            dma((50,)),
             dma((UNITS, 9)),
             dma((UNITS, 9)),
         ],

time: 70.2 us -> 65.4 us (0.932)
  Pallas kernels: 68.2 us -> 63.3 us
    pallas_call x1, Pallas kernels: 68.2 us -> 63.3 us  [shards(): pl.pallas_call(kernel, out_shape=jax.ShapeDtypeStruct((TOKENS, TOKENS), b...]
where the time goes in v3:
time: 65.4 us; the launch traced here: 65.2 us
  Pallas kernels  63.3 us (97%)
  local copies, waits for them, and re-layouts  1.87 us (3%)
    pallas_call x1, Pallas kernels, shards(): pl.pallas_call(kernel, out_shape=jax.ShapeDtypeStruct((TOKENS, TOKENS), b...  63.3 us
    unnamed x1, local copies, waits for them, and re-layouts  1.87 us

profile of v3, /device:TPU:1, one launch (start us, length us, event | category | flops | bytes accessed | tf_op | source)
XLA Modules:
  0.0 65.2 jit_solution(3675688403428790242)
XLA Ops:
  0.0 63.3 %shard_map.82 = bf16[512,512]{1,0:T(8,128)(2,1)} custom-call(s32[4,4]{1,0:T(4,128)} %slash.1, s32[1,2,32]{2,1,0:T(2,128)} %bitcast.11, s32[4,1,32]{2,1,0:T(1,128)} %bitcast.10, s32[4,32]{1,0:T(4,128)} %counts.1, bf16[512,512]{1,0:T(8,128)(2,1)} %q_hbm.1, bf16[8,64,128]{2,1,0:T(8,128)(2,1)} %bitcast.8, bf16[8,64,128]{2,1,0:T(8,128)(2,1)} %bitcast.9, ...), custom_call_target="tpu_custom_call" | custom-call | tf_op jit(solution)/shard_map/pallas_call | solution.py:420
  63.4 1.9 %copy.11 = bf16[512,512]{1,0:T(8,128)(2,1)} copy(bf16[512,512]{1,0:T(8,128)(2,1)} %shard_map.82) | data formatting | bytes 1048576

commit v4 on v3

--- a/solution.py
+++ b/solution.py
@@ -228,26 +228,26 @@
     x_go(along_x, 1, 0)
     z_go(1, 2, 6, 1, 7)
     further(0, 1)
-    further(0, 2)
     q_in.wait()
     previous(ke, 48).wait_recv()
     previous(ve, 49).wait_recv()
     near_rows(0, 1)
+    further(0, 2)
+    near_rows(1, 2)
     further(0, 3)
-    near_rows(1, 2)
+    near_rows(2, 3)
     z_far_go(1)
-    near_rows(2, 3)
+    near_rows(3, 4)
     z_then_x(1, 1, 1, 7)
     further(1, 0)
-    near_rows(3, 4)
+    near_rows(4, 5)
     z_far_come(1)
-    near_rows(4, 5)
+    near_rows(5, 6)
     further(1, 1)
-    near_rows(5, 6)
+    near_rows(6, 7)
     further(1, 2)
-    near_rows(6, 7)
+    near_rows(7, 8)
     further(1, 3)
-    near_rows(7, 8)
     for group in range(4):
         x_come(on_x, 0, group)
 
@@ -305,6 +305,7 @@
                     weights.astype(jnp.bfloat16), vh[at : at + PART, :], preferred_element_type=jnp.float32
                 )
             att[hd, j, rows, :] = (numer / jnp.sum(total, axis=1, keepdims=True)).astype(jnp.bfloat16)
+            y_go(TILES * j + tile, 1, 2, 0)
 
     def source(dy, other=False):
         return lax.rem(y + dy + NY, NY) * 2 + (1 - core if other else core)
@@ -371,7 +372,6 @@
         @pl.when(step < HEADS)
         def _():
             attend(step)
-            of_head(lambda unit: y_go(unit, 1, 2, 0), step)
 
         @pl.when(jnp.logical_or(step == 1, jnp.logical_and(step >= 3, step < HEADS + 2)))
         def _():

time: 65.4 us -> 64.1 us (0.980)
  Pallas kernels: 63.3 us -> 62.1 us
    pallas_call x1, Pallas kernels: 63.3 us -> 62.1 us  [shards(): pl.pallas_call(kernel, out_shape=jax.ShapeDtypeStruct((TOKENS, TOKENS), b...]
where the time goes in v4:
time: 64.1 us; the launch traced here: 64 us
  Pallas kernels  62.1 us (97%)
  local copies, waits for them, and re-layouts  1.87 us (3%)
    pallas_call x1, Pallas kernels, shards(): pl.pallas_call(kernel, out_shape=jax.ShapeDtypeStruct((TOKENS, TOKENS), b...  62.1 us
    unnamed x1, local copies, waits for them, and re-layouts  1.87 us

profile of v4, /device:TPU:1, one launch (start us, length us, event | category | flops | bytes accessed | tf_op | source)
XLA Modules:
  0.0 64.0 jit_solution(2230335916191750305)
XLA Ops:
  0.0 62.1 %shard_map.82 = bf16[512,512]{1,0:T(8,128)(2,1)} custom-call(s32[4,4]{1,0:T(4,128)} %slash.1, s32[1,2,32]{2,1,0:T(2,128)} %bitcast.11, s32[4,1,32]{2,1,0:T(1,128)} %bitcast.10, s32[4,32]{1,0:T(4,128)} %counts.1, bf16[512,512]{1,0:T(8,128)(2,1)} %q_hbm.1, bf16[8,64,128]{2,1,0:T(8,128)(2,1)} %bitcast.8, bf16[8,64,128]{2,1,0:T(8,128)(2,1)} %bitcast.9, ...), custom_call_target="tpu_custom_call" | custom-call | tf_op jit(solution)/shard_map/pallas_call | solution.py:420
  62.1 1.9 %copy.11 = bf16[512,512]{1,0:T(8,128)(2,1)} copy(bf16[512,512]{1,0:T(8,128)(2,1)} %shard_map.82) | data formatting | bytes 1048576
